TPU v7x, 512 devices: a whole 4x8x8 slice. The times are simulated.
512 devices in a mesh: rows: 32 (over z, y_hi, core), protos: 16 (over x, y_lo).
Axes of the slice: x: 4, y: 8 (y_hi: 2, y_lo: 4; y = y_hi * 4 + y_lo), z: 8, core: 2. Of those that a mesh axis runs over, the one named last changes fastest.
Arguments:
- student_patches: bfloat16 [2, 64, 256, 256], P(None, 'rows'), may hold values from -6 to 6
- teacher_patches: bfloat16 [2, 64, 256, 256], P(None, 'rows'), may hold values from -6 to 6
- positions: int32 [2, 64, 64], P(None, 'rows'), may hold values from 0 to 255, as said below
- prototypes: bfloat16 [256, 65536], P('rows', 'protos'), may hold values from -1 to 1
- loss_scale: float32 [1], replicated, may hold values from 327680 to 2621440
Outputs:
- grad_student: float32 [2, 4096, 256], P(None, 'rows', 'protos')
- grad_protos: float32 [256, 65536], P('rows', 'protos')
Inputs may be any that keep to these rules, and one draw needn't show every extreme that they name: Each image's 64 positions are distinct and increasing.
All inputs are finite; a program needn't handle non-finite values.
Results may differ from a plain program's by a relative error of at most 0.027.
Values may be sent and summed in bfloat16 or wider, within the bound.
A program may use at most 64 MiB of HBM per device.

v0:
```python
import jax
import jax.numpy as jnp
from jax import lax
from jax.sharding import PartitionSpec as P

ITERS = 3


teacher_temp = 0.07
student_temp = 0.1
epsilon = 1e-06


def pick_rows(patches, positions):
    picked = jnp.take_along_axis(patches, positions[..., None], axis=2)
    return picked.reshape(picked.shape[0], picked.shape[1] * picked.shape[2], picked.shape[3])


def unit_rows(values):
    widened = values.astype(jnp.float32)
    factor = lax.rsqrt(jnp.sum(widened * widened, axis=-1, keepdims=True) + epsilon)
    return (widened * factor, factor)


def balance(kernel):
    row_scale = jnp.ones(kernel.shape[:2], jnp.float32)
    col_scale = jnp.ones((kernel.shape[0], kernel.shape[2]), jnp.float32)
    for sweep_step in range(ITERS):
        col_part = jnp.sum(row_scale[:, :, None] * kernel, axis=1)
        col_scale = 1.0 / lax.psum(col_part, "rows")
        row_part = jnp.sum(kernel * col_scale[:, None, :], axis=2)
        row_scale = 1.0 / lax.psum(row_part, "protos")
    return (row_scale, col_scale)


def local(student_patches, teacher_patches, positions, prototypes, loss_scale):
    student_rows = pick_rows(student_patches, positions)
    student_unit, student_factor = unit_rows(student_rows)
    teacher_unit = unit_rows(pick_rows(teacher_patches, positions))[0]
    student_half = student_unit.astype(jnp.bfloat16)
    teacher_half = teacher_unit.astype(jnp.bfloat16)
    gathered = lax.all_gather(prototypes, "rows", axis=0, tiled=True)
    proto_wide = gathered.astype(jnp.float32)
    proto_factor = lax.rsqrt(jnp.sum(proto_wide * proto_wide, axis=0, keepdims=True) + epsilon)
    proto_unit = proto_wide * proto_factor
    proto_half = proto_unit.astype(jnp.bfloat16)
    scores = jnp.einsum("mrk,kp->mrp", teacher_half, proto_half, preferred_element_type=jnp.float32)
    kernel = jnp.exp(scores / teacher_temp)
    results = [balance(kernel[member : member + 1]) for member in range(kernel.shape[0])]
    row_scale = jnp.concatenate([result[0] for result in results], axis=0)
    col_scale = jnp.concatenate([result[1] for result in results], axis=0)
    targets = row_scale[:, :, None] * kernel * col_scale[:, None, :]
    logits = (
        jnp.einsum("mrk,kp->mrp", student_half, proto_half, preferred_element_type=jnp.float32)
        / student_temp
    )
    exponent = jnp.exp(logits)
    totals = lax.psum(jnp.sum(exponent, axis=2), "protos")
    row_count = kernel.shape[0] * kernel.shape[1] * lax.axis_size("rows")
    factor_scale = loss_scale[0] / (row_count * student_temp)
    slopes = ((exponent / totals[:, :, None] - targets) * factor_scale).astype(jnp.bfloat16)
    feature_grad = jnp.einsum("mrp,kp->mrk", slopes, proto_half, preferred_element_type=jnp.float32)
    col_width = student_rows.shape[2] // lax.axis_size("protos")
    first_col = lax.axis_index("protos") * col_width
    summed = lax.psum(feature_grad.astype(jnp.bfloat16), "protos").astype(jnp.float32)
    inner_dot = jnp.sum(student_unit * summed, axis=2, keepdims=True)
    full_grad = (summed - student_unit * inner_dot) * student_factor
    grad_student = lax.dynamic_slice_in_dim(full_grad, first_col, col_width, 2)
    proto_sum = jnp.einsum("mrk,mrp->kp", student_half, slopes, preferred_element_type=jnp.float32)
    column_dot = jnp.sum(proto_unit * proto_sum, axis=0, keepdims=True)
    proto_term = (proto_sum - proto_unit * column_dot) * proto_factor
    height = prototypes.shape[0]
    summed_protos = lax.psum(proto_term.astype(jnp.bfloat16), "rows").astype(jnp.float32)
    grad_protos = lax.dynamic_slice_in_dim(
        summed_protos, lax.axis_index("rows") * height, height, 0
    )
    return (grad_student, grad_protos)


def solution(mesh):
    in_specs = (
        P(None, "rows", None, None),
        P(None, "rows", None, None),
        P(None, "rows", None),
        P("rows", "protos"),
        P(),
    )
    out_specs = (P(None, "rows", "protos"), P("rows", "protos"))
    return jax.shard_map(local, mesh=mesh, in_specs=in_specs, out_specs=out_specs, check_vma=False)
```

profile of v0, /device:TPU:1, one launch (start us, length us, event | category | flops | bytes accessed | tf_op | source)
XLA Modules:
  0.0 1695.6 jit_solution(761851111689257239)
XLA Ops:
  8.8 1.9 gather_fusion
  10.7 1.9 gather_fusion.1
  14.0 93.7 %all-gather.2.cloned.1.call-done = bf16[256,4096]{1,0:T(8,128)(2,1)} async-done(((bf16[8,4096]{1,0:T(8,128)(2,1)}), bf16[256,4096]{1,0:T(8,128)(2,1)}) %all-gather.2.cloned.1.call-update) | async-done | bytes 2097168 | tf_op jit(solution)/shard_map/all_gather | solution.py:42
  107.7 2.2 fusion.9
  110.9 1.9 copy-done.1
  112.9 160.2 %psum.106 = f32[1,4096]{1,0:T(1,128)S(1)} all-reduce(f32[1,4096]{1,0:T(1,128)S(1)} %bitcast.73), channel_id=1, replica_groups=mesh['rows'=32,'protos'=16] {'rows'}, use_global_device_ids=true, to_apply=%region_6.0 | all-reduce | flops 4096 | bytes 32768 | tf_op jit(solution)/shard_map/psum | solution.py:30
  275.0 36.5 %psum.107 = f32[1,128]{1,0:T(1,128)S(1)} all-reduce(f32[1,128]{1,0:T(1,128)S(1)} %bitcast.77), channel_id=1, replica_groups=mesh['rows'=32,'protos'=16] {'protos'}, use_global_device_ids=true, to_apply=%region_8.0 | all-reduce | flops 128 | bytes 1024 | tf_op jit(solution)/shard_map/psum | solution.py:32
  313.4 174.2 %psum.108 = f32[1,4096]{1,0:T(1,128)S(1)} all-reduce(f32[1,4096]{1,0:T(1,128)S(1)} %bitcast.68), channel_id=1, replica_groups=mesh['rows'=32,'protos'=16] {'rows'}, use_global_device_ids=true, to_apply=%region_10.0 | all-reduce | flops 4096 | bytes 32768 | tf_op jit(solution)/shard_map/psum | solution.py:30
  489.4 31.0 %psum.109 = f32[1,128]{1,0:T(1,128)S(1)} all-reduce(f32[1,128]{1,0:T(1,128)S(1)} %bitcast.78), channel_id=1, replica_groups=mesh['rows'=32,'protos'=16] {'protos'}, use_global_device_ids=true, to_apply=%region_12.0 | all-reduce | flops 128 | bytes 1024 | tf_op jit(solution)/shard_map/psum | solution.py:32
  520.5 2.6 multiply_reduce_fusion.6
  523.1 174.0 %all-reduce = (f32[1,4096]{1,0:T(1,128)S(1)}, f32[1,4096]{1,0:T(1,128)S(1)}) all-reduce(f32[1,4096]{1,0:T(1,128)S(1)} %bitcast.64, f32[1,4096]{1,0:T(1,128)S(1)} %bitcast.65), channel_id=1, replica_groups=mesh['rows'=32,'protos'=16] {'rows'}, use_global_device_ids=true, to_apply=%region_14.0 | all-reduce | flops 8192 | bytes 65536 | tf_op jit(solution)/shard_map/psum | solution.py:30
  697.1 2.6 multiply_reduce_fusion.5
  699.7 32.7 %psum.113 = f32[1,128]{1,0:T(1,128)S(1)} all-reduce(f32[1,128]{1,0:T(1,128)S(1)} %bitcast.76), channel_id=1, replica_groups=mesh['rows'=32,'protos'=16] {'protos'}, use_global_device_ids=true, to_apply=%region_20.0 | all-reduce | flops 128 | bytes 1024 | tf_op jit(solution)/shard_map/psum | solution.py:32
  734.3 174.2 %psum.114 = f32[1,4096]{1,0:T(1,128)S(1)} all-reduce(f32[1,4096]{1,0:T(1,128)S(1)} %bitcast.70), channel_id=1, replica_groups=mesh['rows'=32,'protos'=16] {'rows'}, use_global_device_ids=true, to_apply=%region_22.0 | all-reduce | flops 4096 | bytes 32768 | tf_op jit(solution)/shard_map/psum | solution.py:30
  908.6 1.8 multiply_reduce_fusion.2
  910.4 31.0 %psum.115 = f32[1,128]{1,0:T(1,128)S(1)} all-reduce(f32[1,128]{1,0:T(1,128)S(1)} %bitcast.79), channel_id=1, replica_groups=mesh['rows'=32,'protos'=16] {'protos'}, use_global_device_ids=true, to_apply=%region_24.0 | all-reduce | flops 128 | bytes 1024 | tf_op jit(solution)/shard_map/psum | solution.py:32
  943.3 174.0 %psum.116 = f32[1,4096]{1,0:T(1,128)S(1)} all-reduce(f32[1,4096]{1,0:T(1,128)S(1)} %bitcast.72), channel_id=1, replica_groups=mesh['rows'=32,'protos'=16] {'rows'}, use_global_device_ids=true, to_apply=%region_26.0 | all-reduce | flops 4096 | bytes 32768 | tf_op jit(solution)/shard_map/psum | solution.py:30
  1119.2 3.0 fusion.18
  1122.2 32.9 %all-reduce.1 = (f32[1,128]{1,0:T(1,128)S(1)}, f32[1,128]{1,0:T(1,128)S(1)}, f32[2,128]{1,0:T(2,128)S(1)}) all-reduce(f32[1,128]{1,0:T(1,128)S(1)} %bitcast.75, f32[1,128]{1,0:T(1,128)S(1)} %bitcast.74, f32[2,128]{1,0:T(2,128)S(1)} %get-tuple-element.18), channel_id=1, replica_groups=mesh['rows'=32,'protos'=16] {'protos'}, use_global_device_ids=true, to_apply=%region_28.0 | all-reduce | flops 512 | bytes 4096 | tf_op jit(solution)/shard_map/psum | solution.py:32
  1155.1 4.7 multiply_convert_fusion
  1162.8 2.5 fusion.5
  1165.3 2.1 fusion.8
  1167.4 156.3 %all-reduce.5.cloned.1.call-done = bf16[2,128,256]{2,1,0:T(8,128)(2,1)} async-done(((bf16[2,128,256]{2,1,0:T(8,128)(2,1)}), bf16[2,128,256]{2,1,0:T(8,128)(2,1)}) %all-reduce.5.cloned.1.call-update) | async-done | bytes 131088 | tf_op jit(solution)/shard_map/psum | solution.py:65
  1326.5 361.0 %all-reduce.7.cloned.1.call-done = bf16[256,4096]{1,0:T(8,128)(2,1)} async-done(((bf16[256,4096]{1,0:T(8,128)(2,1)}), bf16[256,4096]{1,0:T(8,128)(2,1)}) %all-reduce.7.cloned.1.call-update) | async-done | bytes 2097168 | tf_op jit(solution)/shard_map/psum | solution.py:73
  (56 shorter events, 21.9 us)
Async XLA Ops:
  7.2 1.6 copy-start
  7.2 5.5 copy-start.5
  7.2 3.5 copy-start.4
  7.2 100.5 %all-gather.2.cloned.1.call-start = ((), (), s32[]{:S(2)}) async-start(), calls=%async_computation | async-start | bytes 2162688 | tf_op jit(solution)/shard_map/all_gather | solution.py:42
  7.9 1315.8 %all-reduce.5.cloned.1.call-start = ((), (), s32[]{:S(2)}) async-start(), calls=%async_computation.1 | async-start | bytes 262144 | tf_op jit(solution)/shard_map/psum | solution.py:65
  107.7 2.2 copy-start.2
  110.9 1.9 copy-start.1
  1159.8 1.4 copy-start.3
  1162.7 524.8 %all-reduce.7.cloned.1.call-start = ((), (), s32[]{:S(2)}) async-start(), calls=%async_computation.2 | async-start | bytes 4194304 | tf_op jit(solution)/shard_map/psum | solution.py:73
Sparse Core Ops, SparseCore 0:
  11.4 96.2 all-gather.1
  1162.9 160.8 all-reduce.4
  1326.9 360.6 all-reduce.6
where the time goes:
time: 1700 us
  blocking collectives  1020 us (60%)
  waiting for transfers between devices  612 us (36%)
  other arithmetic  32.3 us (2%)
    psum x5, blocking collectives, balance(): col_scale = 1.0 / lax.psum(col_part, 'rows')  857 us
    psum x1, waiting for transfers between devices, local(): lax.psum(proto_term.astype(jnp.bfloat16), 'rows').astype(jnp.float32)  361 us
    psum x5, blocking collectives, balance(): row_scale = 1.0 / lax.psum(row_part, 'protos')  164 us
    psum x1, waiting for transfers between devices, local(): lax.psum(feature_grad.astype(jnp.bfloat16), 'protos').astype(jnp.float32)  156 us
    all_gather x1, waiting for transfers between devices, local(): gathered = lax.all_gather(prototypes, 'rows', axis=0, tiled=True)  93.7 us
  transfers between devices with their start and end apart: 3, of which 3 were waited for; matrix products, arithmetic and copies ran while one was open for 1% of the time, Pallas kernels for 0%

commit v1 on v0

v1 whole, which is shorter than its diff:
```python
import math

import jax
import jax.numpy as jnp
from jax import lax
from jax.experimental import pallas as pl
from jax.experimental.pallas import tpu as pltpu
from jax.sharding import PartitionSpec as P

ITERS = 3
LOG2E = 1.4426950408889634
TEACHER_EXP2 = LOG2E / 0.07
STUDENT_EXP2 = LOG2E / 0.1
EPSILON = 1e-6
MESH = pl.DeviceIdType.MESH
F32 = jnp.float32
BF16 = jnp.bfloat16


def dot(a, b, ca, cb):
    return lax.dot_general(a, b, (((ca,), (cb,)), ((), ())), preferred_element_type=F32)


def kernel(
    sp_hbm, tp_hbm, pos_ref, pr_ref, scale_ref,
    gs_ref, gp_ref,
    sp, tp, send_p, pg, pu, ph, pfac,
    tx, sx, th, sh, sht, ut, sfac,
    kmat, emat, slopes,
    colbuf, rowbuf1, rowbuf2, csc, rb, tb,
    send_r, rr, pterm, fs, fr, gsend, grecv,
    local_sem, pg_send, pg_recv,
    tx_send, tx_recv, sx_send, sx_recv,
    col_send, col_recv, row1_send, row1_recv, row2_send, row2_recv,
    rr_send, rr_recv, fr_send, fr_recv, gr_send, gr_recv,
):
    me = lax.axis_index("rows")
    mp = lax.axis_index("protos")
    z, h, c = me // 4, lax.rem(me // 2, 2), lax.rem(me, 2)
    x, l = mp // 4, lax.rem(mp, 4)
    q = h * 2 + c
    y = h * 4 + l

    def rows_dev(d):
        return (lax.rem(me + d, 32), mp)

    def z_dev(d):
        return (lax.rem(z + d, 8) * 4 + q, mp)

    def cx_dev(i):
        dx, dc = i // 2, lax.rem(i, 2)
        return (z * 4 + h * 2 + lax.rem(c + dc, 2), lax.rem(x + dx, 4) * 4 + l)

    def y_dev(d):
        other = lax.rem(y + d, 8)
        return (z * 4 + (other // 4) * 2 + c, x * 4 + lax.rem(other, 4))

    barrier = pltpu.get_barrier_semaphore()

    def greet(group, count):
        def body(d, carry):
            pl.semaphore_signal(barrier, inc=1, device_id=group(d), device_id_type=MESH)
            return carry
        lax.fori_loop(1, count, body, 0)

    greet(rows_dev, 32)
    greet(cx_dev, 8)
    greet(y_dev, 8)

    load_t = pltpu.make_async_copy(tp_hbm, tp, local_sem.at[0])
    load_t.start()
    load_s = pltpu.make_async_copy(sp_hbm, sp, local_sem.at[1])
    load_s.start()

    wide = pr_ref[...].astype(F32)
    for other in range(4):
        first = wide[:, other * 1024 : other * 1024 + 512]
        second = wide[:, other * 1024 + 512 : other * 1024 + 1024]
        send_p[other] = jnp.concatenate([first, second], axis=0).astype(BF16)
    pg[pl.ds(me, 1)] = send_p[pl.ds(q, 1)]

    pl.semaphore_wait(barrier, 45)

    def send_proto(d, carry):
        target = lax.rem(me + d, 32)
        pltpu.make_async_remote_copy(
            send_p.at[lax.rem(target, 4)], pg.at[me], pg_send.at[d], pg_recv.at[d],
            device_id=(target, mp), device_id_type=MESH,
        ).start()
        return carry

    lax.fori_loop(1, 32, send_proto, 0)

    def pick(patches, m):
        parts = []
        for image in range(2):
            where = jnp.broadcast_to(pos_ref[m, image : image + 1, :], (256, 64))
            hot = (lax.broadcasted_iota(jnp.int32, (256, 64), 0) == where).astype(F32).astype(BF16)
            parts.append(dot(hot, patches[m, image], 0, 0))
        return jnp.concatenate(parts, axis=0).astype(BF16)

    core_dev = (z * 4 + h * 2 + (1 - c), mp)
    y4_dev = (z * 4 + (1 - h) * 2 + c, mp)
    q_far = (1 - h) * 2 + c
    mine = pl.ds(pl.multiple_of(x * 32, 32), 32)

    def far_copy(buf, send, recv, i):
        return pltpu.make_async_remote_copy(
            buf.at[:, q_far, mine], buf.at[:, q_far, mine], send.at[i], recv.at[i],
            device_id=cx_dev(i), device_id_type=MESH,
        )

    def y4_copy(buf, send, recv):
        return pltpu.make_async_remote_copy(
            buf.at[:, q, mine], buf.at[:, q, mine], send.at[8], recv.at[8],
            device_id=y4_dev, device_id_type=MESH,
        )

    def core_copy(buf, send, recv):
        return pltpu.make_async_remote_copy(
            buf.at[:, q], buf.at[:, q], send.at[0], recv.at[0],
            device_id=core_dev, device_id_type=MESH,
        )

    load_t.wait()
    for m in range(2):
        tx[m, pl.ds(q, 1)] = pick(tp, m)[None]
    y4_copy(tx, tx_send, tx_recv).start()
    core_copy(tx, tx_send, tx_recv).start()
    load_s.wait()
    for m in range(2):
        sx[m, pl.ds(q, 1)] = pick(sp, m)[None]
    y4_copy(sx, sx_send, sx_recv).start()
    core_copy(sx, sx_send, sx_recv).start()

    def forward_far(buf, send, recv):
        y4_copy(buf, send, recv).wait_recv()

        def body(i, carry):
            far_copy(buf, send, recv, i).start()
            return carry

        lax.fori_loop(1, 8, body, 0)

    def rows_arrive(buf, send, recv):
        core_copy(buf, send, recv).wait_recv()

        def body(i, carry):
            far_copy(buf, send, recv, i).wait_recv()
            return carry

        lax.fori_loop(1, 8, body, 0)

    def rows_sent(buf, send, recv):
        y4_copy(buf, send, recv).wait_send()
        core_copy(buf, send, recv).wait_send()

        def body(i, carry):
            far_copy(buf, send, recv, i).wait_send()
            return carry

        lax.fori_loop(1, 8, body, 0)

    forward_far(tx, tx_send, tx_recv)
    forward_far(sx, sx_send, sx_recv)

    rows_arrive(tx, tx_send, tx_recv)
    for m in range(2):
        for part in range(4):
            values = tx[m, part].astype(F32)
            factor = lax.rsqrt(jnp.sum(values * values, axis=1, keepdims=True) + EPSILON)
            th[m, part * 128 : part * 128 + 128, :] = (values * factor).astype(BF16)

    rows_arrive(sx, sx_send, sx_recv)
    for m in range(2):
        for part in range(4):
            values = sx[m, part].astype(F32)
            turned = jnp.concatenate([values[:, :128].T, values[:, 128:].T], axis=0)
            factor = lax.rsqrt(jnp.sum(turned * turned, axis=0, keepdims=True) + EPSILON)
            unit = turned * factor
            at = slice(part * 128, part * 128 + 128)
            ut[m, :, at] = unit
            sht[m, :, at] = unit.astype(BF16)
            sfac[m, part] = jnp.broadcast_to(factor, (8, 128))
            sh[m, at, :] = jnp.concatenate([unit[:128, :].T, unit[128:, :].T], axis=1).astype(BF16)

    def wait_proto(d, carry):
        pltpu.make_async_remote_copy(
            send_p.at[0], pg.at[me], pg_send.at[d], pg_recv.at[d],
            device_id=rows_dev(d), device_id_type=MESH,
        ).wait_recv()
        return carry

    lax.fori_loop(1, 32, wait_proto, 0)

    def unpack(b, total):
        block = pg[b].astype(F32)
        rows = jnp.concatenate([block[0:8, :], block[8:16, :]], axis=1)
        pu[pl.ds(pl.multiple_of(b * 8, 8), 8), :] = rows
        return total + rows * rows

    total = lax.fori_loop(0, 32, unpack, jnp.zeros((8, 1024), F32))
    pfac[...] = jnp.broadcast_to(
        lax.rsqrt(jnp.sum(total, axis=0, keepdims=True) + EPSILON), (8, 1024)
    )

    def normalize(b, carry):
        at = pl.ds(pl.multiple_of(b * 16, 16), 16)
        unit = pu[at, :] * pfac[0:1, :]
        pu[at, :] = unit
        ph[at, :] = unit.astype(BF16)
        return carry

    lax.fori_loop(0, 16, normalize, 0)

    def tile_send(buf, send, recv, group):
        def body(d, carry):
            pltpu.make_async_remote_copy(
                buf.at[0], buf.at[d], send.at[d], recv.at[d], device_id=group(d), device_id_type=MESH
            ).start()
            return carry
        lax.fori_loop(1, 8, body, 0)

    def tile_recv(buf, send, recv, group):
        def body(d, carry):
            pltpu.make_async_remote_copy(
                buf.at[0], buf.at[d], send.at[d], recv.at[d], device_id=group(d), device_id_type=MESH
            ).wait_recv()
            return carry
        lax.fori_loop(1, 8, body, 0)
        return jnp.sum(buf[...], axis=0)

    def col_store(it, m, tile, sums):
        width = sums.shape[1] // 128
        for part in range(width):
            row = tile * width + part
            colbuf[it, m, 0, row : row + 1, :] = sums[:, part * 128 : part * 128 + 128]

    def lane_sums(block):
        return jnp.sum(block.T, axis=0, keepdims=True)

    def spread(row):
        return jnp.broadcast_to(row, (128, 128)).T

    def col_send_start(it, m):
        tile_send(colbuf.at[it, m], col_send.at[it, m], col_recv.at[it, m], z_dev)

    for m in range(2):
        for tile in range(4):
            at = slice(tile * 256, tile * 256 + 256)
            scores = dot(th[m], ph[:, at], 1, 0)
            values = jnp.exp2(scores * TEACHER_EXP2)
            kmat[m, :, at] = values
            col_store(0, m, tile, jnp.sum(values, axis=0, keepdims=True))
        col_send_start(0, m)

    for m in range(2):
        acc = None
        for tile in range(4):
            at = slice(tile * 256, tile * 256 + 256)
            logits = dot(sh[m], ph[:, at], 1, 0)
            values = jnp.exp2(logits * STUDENT_EXP2)
            emat[m, :, at] = values
            half = values[:, :128] + values[:, 128:]
            acc = half if acc is None else acc + half
        for part in range(4):
            rowbuf1[0, m, 0, 4 + part : 5 + part, :] = lane_sums(acc[part * 128 : part * 128 + 128, :])

    loss_factor = scale_ref[0] * (1.0 / (2 * 4096 * 0.1))

    for it in range(ITERS):
        for m in range(2):
            total = tile_recv(colbuf.at[it, m], col_send.at[it, m], col_recv.at[it, m], z_dev)
            csc[m] = 1.0 / total
            for part in range(4):
                at = slice(part * 128, part * 128 + 128)
                acc = jnp.zeros((128, 128), F32)
                for tile in range(8):
                    acc = acc + kmat[m, at, tile * 128 : tile * 128 + 128] * csc[m, tile : tile + 1, :]
                rowbuf1[it, m, 0, part : part + 1, :] = lane_sums(acc)
            if it > 0:
                rowbuf1[it, m, 0, 4:8, :] = jnp.zeros((4, 128), F32)
            tile_send(rowbuf1.at[it, m], row1_send.at[it, m], row1_recv.at[it, m], cx_dev)
        for m in range(2):
            total = tile_recv(rowbuf1.at[it, m], row1_send.at[it, m], row1_recv.at[it, m], cx_dev)
            rowbuf2[it, m, 0] = total
            tile_send(rowbuf2.at[it, m], row2_send.at[it, m], row2_recv.at[it, m], y_dev)
        for m in range(2):
            total = tile_recv(rowbuf2.at[it, m], row2_send.at[it, m], row2_recv.at[it, m], y_dev)
            inverse = 1.0 / total[0:4, :]
            if it == ITERS - 1:
                inverse = inverse * loss_factor
            for part in range(4):
                rb[m, part * 128 : part * 128 + 128, :] = spread(inverse[part : part + 1, :])
            if it == 0:
                denominator = loss_factor / total[4:8, :]
                for part in range(4):
                    tb[m, part * 128 : part * 128 + 128, :] = spread(denominator[part : part + 1, :])
            if it < ITERS - 1:
                for tile in range(8):
                    at = slice(tile * 128, tile * 128 + 128)
                    sums = jnp.sum(kmat[m, :, at] * rb[m], axis=0, keepdims=True)
                    col_store(it + 1, m, tile, sums)
                col_send_start(it + 1, m)

    for m in range(2):
        for tile in range(8):
            at = slice(tile * 128, tile * 128 + 128)
            target = kmat[m, :, at] * rb[m] * csc[m, tile : tile + 1, :]
            slopes[m, :, at] = (emat[m, :, at] * tb[m] - target).astype(BF16)

    for tile in range(4):
        at = slice(tile * 256, tile * 256 + 256)
        proto_sum = dot(sht[0], slopes[0, :, at], 1, 0) + dot(sht[1], slopes[1, :, at], 1, 0)
        unit = pu[:, at]
        column_dot = jnp.sum(unit * proto_sum, axis=0, keepdims=True)
        pterm[:, at] = (proto_sum - unit * column_dot) * pfac[0:1, at]

    def send_back(d, carry):
        target = lax.rem(me + d, 32)
        rows = pterm[pl.ds(pl.multiple_of(target * 8, 8), 8), :]
        packed = jnp.concatenate([rows[:, :512], rows[:, 512:]], axis=0)
        send_r[pl.ds(d, 1)] = packed.astype(BF16)[None]
        pltpu.make_async_remote_copy(
            send_r.at[d], rr.at[me], rr_send.at[d], rr_recv.at[d],
            device_id=(target, mp), device_id_type=MESH,
        ).start()
        return carry

    lax.fori_loop(1, 32, send_back, 0)
    own = pterm[pl.ds(pl.multiple_of(me * 8, 8), 8), :]
    rr[pl.ds(me, 1)] = jnp.concatenate([own[:, :512], own[:, 512:]], axis=0).astype(BF16)[None]

    for m in range(2):
        grad = dot(ph[...], slopes[m], 1, 1)
        unit = ut[m]
        inner = jnp.sum(unit * grad, axis=0, keepdims=True)
        grad = (grad - unit * inner).astype(BF16)
        for xx in range(4):
            for part in range(4):
                lane = ((part // 2) * 2 + m) * 128
                fs[xx * 2 + part % 2, :, lane : lane + 128] = grad[
                    xx * 64 : xx * 64 + 64, part * 128 : part * 128 + 128
                ]

    def fs_copy(i):
        slot = lax.rem(x + i // 2, 4) * 2 + lax.rem(c + lax.rem(i, 2), 2)
        return pltpu.make_async_remote_copy(
            fs.at[slot], fr.at[i], fr_send.at[i], fr_recv.at[i],
            device_id=cx_dev(i), device_id_type=MESH,
        )

    def fs_start(i, carry):
        fs_copy(i).start()
        return carry

    def fs_wait(i, carry):
        fs_copy(i).wait_recv()
        return carry

    lax.fori_loop(1, 8, fs_start, 0)
    fr[pl.ds(0, 1)] = fs[pl.ds(x * 2 + c, 1)]
    lax.fori_loop(1, 8, fs_wait, 0)

    def fs_sum(l_to, carry):
        at = pl.ds(pl.multiple_of(l_to * 16, 16), 16)
        total = fr[0, at, :].astype(F32)
        for slot in range(1, 8):
            total = total + fr[slot, at, :].astype(F32)
        total = total.astype(BF16)
        gsend[pl.ds(l_to, 1)] = total[:, :256][None]
        gsend[pl.ds(4 + l_to, 1)] = total[:, 256:][None]
        return carry

    lax.fori_loop(0, 4, fs_sum, 0)

    def gr_copy(d):
        return pltpu.make_async_remote_copy(
            gsend.at[lax.rem(y + d, 8)], grecv.at[d], gr_send.at[d], gr_recv.at[d],
            device_id=y_dev(d), device_id_type=MESH,
        )

    def gr_start(d, carry):
        gr_copy(d).start()
        return carry

    def gr_wait(d, carry):
        gr_copy(d).wait_recv()
        return carry

    lax.fori_loop(1, 8, gr_start, 0)
    grecv[pl.ds(0, 1)] = gsend[pl.ds(y, 1)]
    lax.fori_loop(1, 8, gr_wait, 0)
    total = jnp.sum(grecv[...].astype(F32), axis=0)
    for m in range(2):
        gs_ref[:, m * 128 : m * 128 + 128] = (
            total[:, m * 128 : m * 128 + 128] * sfac[m, pl.ds(q, 1)][0, 0:1, :]
        )

    def rr_copy(d):
        return pltpu.make_async_remote_copy(
            send_r.at[d], rr.at[me], rr_send.at[d], rr_recv.at[d],
            device_id=rows_dev(d), device_id_type=MESH,
        )

    def rr_wait(d, carry):
        rr_copy(d).wait_recv()
        return carry

    lax.fori_loop(1, 32, rr_wait, 0)
    for part in range(4):
        total = rr[part].astype(F32)
        for zz in range(1, 8):
            total = total + rr[zz * 4 + part].astype(F32)
        gp_ref[:, part * 1024 : part * 1024 + 512] = total[0:8, :]
        gp_ref[:, part * 1024 + 512 : part * 1024 + 1024] = total[8:16, :]

    rows_sent(tx, tx_send, tx_recv)
    rows_sent(sx, sx_send, sx_recv)

    def drain31(d, carry):
        pltpu.make_async_remote_copy(
            send_p.at[0], pg.at[me], pg_send.at[d], pg_recv.at[d],
            device_id=rows_dev(d), device_id_type=MESH,
        ).wait_send()
        rr_copy(d).wait_send()
        return carry

    lax.fori_loop(1, 32, drain31, 0)

    def drain7(d, carry):
        fs_copy(d).wait_send()
        gr_copy(d).wait_send()
        for it in range(ITERS):
            for m in range(2):
                for buf, send, recv, group in (
                    (colbuf, col_send, col_recv, z_dev),
                    (rowbuf1, row1_send, row1_recv, cx_dev),
                    (rowbuf2, row2_send, row2_recv, y_dev),
                ):
                    pltpu.make_async_remote_copy(
                        buf.at[it, m, 0], buf.at[it, m, d], send.at[it, m, d], recv.at[it, m, d],
                        device_id=group(d), device_id_type=MESH,
                    ).wait_send()
        return carry

    lax.fori_loop(1, 8, drain7, 0)


def local(student_patches, teacher_patches, positions, prototypes, loss_scale):
    vmem = pl.BlockSpec(memory_space=pltpu.VMEM)
    dma = pltpu.SemaphoreType.DMA
    grad_t, grad_protos = pl.pallas_call(
        kernel,
        out_shape=(
            jax.ShapeDtypeStruct((16, 256), F32),
            jax.ShapeDtypeStruct((8, 4096), F32),
        ),
        in_specs=[
            pl.BlockSpec(memory_space=pl.ANY),
            pl.BlockSpec(memory_space=pl.ANY),
            vmem,
            vmem,
            pl.BlockSpec(memory_space=pltpu.SMEM),
        ],
        out_specs=(vmem, vmem),
        scratch_shapes=[
            pltpu.VMEM((2, 2, 256, 256), BF16),
            pltpu.VMEM((2, 2, 256, 256), BF16),
            pltpu.VMEM((4, 16, 512), BF16),
            pltpu.VMEM((32, 16, 512), BF16),
            pltpu.VMEM((256, 1024), F32),
            pltpu.VMEM((256, 1024), BF16),
            pltpu.VMEM((8, 1024), F32),
            pltpu.VMEM((2, 4, 128, 256), BF16),
            pltpu.VMEM((2, 4, 128, 256), BF16),
            pltpu.VMEM((2, 512, 256), BF16),
            pltpu.VMEM((2, 512, 256), BF16),
            pltpu.VMEM((2, 256, 512), BF16),
            pltpu.VMEM((2, 256, 512), F32),
            pltpu.VMEM((2, 4, 8, 128), F32),
            pltpu.VMEM((2, 512, 1024), F32),
            pltpu.VMEM((2, 512, 1024), F32),
            pltpu.VMEM((2, 512, 1024), BF16),
            pltpu.VMEM((ITERS, 2, 8, 8, 128), F32),
            pltpu.VMEM((ITERS, 2, 8, 8, 128), F32),
            pltpu.VMEM((ITERS, 2, 8, 8, 128), F32),
            pltpu.VMEM((2, 8, 128), F32),
            pltpu.VMEM((2, 512, 128), F32),
            pltpu.VMEM((2, 512, 128), F32),
            pltpu.VMEM((32, 16, 512), BF16),
            pltpu.VMEM((32, 16, 512), BF16),
            pltpu.VMEM((256, 1024), F32),
            pltpu.VMEM((8, 64, 512), BF16),
            pltpu.VMEM((8, 64, 512), BF16),
            pltpu.VMEM((8, 16, 256), BF16),
            pltpu.VMEM((8, 16, 256), BF16),
            dma((2,)),
            dma((32,)),
            dma((32,)),
            dma((9,)),
            dma((9,)),
            dma((9,)),
            dma((9,)),
            dma((ITERS, 2, 8)),
            dma((ITERS, 2, 8)),
            dma((ITERS, 2, 8)),
            dma((ITERS, 2, 8)),
            dma((ITERS, 2, 8)),
            dma((ITERS, 2, 8)),
            dma((32,)),
            dma((32,)),
            dma((8,)),
            dma((8,)),
            dma((8,)),
            dma((8,)),
        ],
        compiler_params=pltpu.CompilerParams(
            collective_id=0, has_side_effects=True, vmem_limit_bytes=48 * 2**20
        ),
        cost_estimate=pl.CostEstimate(
            flops=2_200_000_000, bytes_accessed=2_000_000, transcendentals=2_000_000
        ),
        name="ibot_head",
    )(student_patches, teacher_patches, positions, prototypes, loss_scale)
    grad_student = jnp.transpose(grad_t.reshape(16, 2, 128), (1, 2, 0))
    return grad_student, grad_protos


def solution(mesh):
    in_specs = (
        P(None, "rows", None, None),
        P(None, "rows", None, None),
        P(None, "rows", None),
        P("rows", "protos"),
        P(),
    )
    out_specs = (P(None, "rows", "protos"), P("rows", "protos"))
    return jax.shard_map(local, mesh=mesh, in_specs=in_specs, out_specs=out_specs, check_vma=False)
```

time: 1700 us -> 115 us (0.07)
  blocking collectives: 1020 us -> 0 us
  waiting for transfers between devices: 612 us -> 0 us
  Pallas kernels: 0 us -> 109 us
  other arithmetic: 32.3 us -> 0 us
    psum x10 -> x0, blocking collectives: 1020 us -> none  [the longest x5 857 us: balance(): col_scale = 1.0 / lax.psum(col_part, 'rows')]
    psum x2 -> x0, waiting for transfers between devices: 517 us -> none  [the longest x1 361 us: local(): lax.psum(proto_term.astype(jnp.bfloat16), 'rows').astype(jnp.float32)]
    pallas_call x0 -> x1, Pallas kernels: none -> 109 us  [local(): pl.pallas_call(kernel, out_shape=(jax.ShapeDtypeStruct((16, 256), F32), j...]
    all_gather x1 -> x0, waiting for transfers between devices: 93.7 us -> none  [local(): gathered = lax.all_gather(prototypes, 'rows', axis=0, tiled=True)]
    reduce_sum x13 -> x0, other arithmetic: 21.7 us -> none  [the longest x5 10 us: balance(): row_part = jnp.sum(kernel * col_scale[:, None, :], axis=2)]
  transfers between devices with their start and end apart: 3 -> 0, of which waited for: 3 -> 0; matrix products, arithmetic and copies ran while one was open for 1% -> 0% of each run, Pallas kernels for 0% -> 0%
where the time goes in v1:
time: 115 us
  Pallas kernels  109 us (95%)
  local copies, waits for them, and re-layouts  4.86 us (4%)
  between operations  1.3 us (1%)
    pallas_call x1, Pallas kernels, local(): pl.pallas_call(kernel, out_shape=(jax.ShapeDtypeStruct((16, 256), F32), j...  109 us
    unnamed x9, local copies, waits for them, and re-layouts  4.25 us

profile of v1, /device:TPU:1, one launch (start us, length us, event | category | flops | bytes accessed | tf_op | source)
XLA Modules:
  0.0 115.2 jit_solution(6435228690583459205)
XLA Ops:
  1.3 0.0 copy-start
  1.3 1.0 copy-done
  2.3 0.0 copy-start.1
  2.3 1.0 copy-done.1
  3.4 0.0 copy-start.2
  3.4 0.8 copy-done.2
  4.2 0.0 copy-start.3
  4.2 0.7 copy-done.3
  4.9 109.0 %ibot_head.1 = (f32[16,256]{1,0:T(8,128)S(1)}, f32[8,4096]{1,0:T(8,128)S(1)}) custom-call(bf16[2,2,256,256]{3,2,1,0:T(8,128)(2,1)S(1)} %copy-done, bf16[2,2,256,256]{3,2,1,0:T(8,128)(2,1)S(1)} %copy-done.1, s32[2,2,64]{2,1,0:T(2,128)S(1)} %copy-done.3, bf16[8,4096]{1,0:T(8,128)(2,1)S(1)} %copy-done.2, f32[1]{0:T(128)S(6)} %copy.11.scale_ref), custom_call_target="tpu_custom_call" | custom-call | flops 2200000000 | bytes 2000000 | tf_op jit(solution)/shard_map/ibot_head/pallas_call | solution.py:453
  113.9 0.6 bitcast_bitcast_fusion
  114.5 0.7 copy.12
Async XLA Ops:
  1.3 1.0 copy-start
  2.3 1.0 copy-start.1
  3.4 0.8 copy-start.2
  4.2 0.7 copy-start.3

commit v2 on v1

--- a/solution.py
+++ b/solution.py
@@ -22,9 +22,9 @@
 
 
 def kernel(
-    sp_hbm, tp_hbm, pos_ref, pr_ref, scale_ref,
+    sp_hbm, tp_hbm, pos_hbm, pr_hbm, scale_hbm,
     gs_ref, gp_ref,
-    sp, tp, send_p, pg, pu, ph, pfac,
+    sp, tp, pos_ref, pr_ref, scale_ref, send_p, pg, pu, ph, pfac,
     tx, sx, th, sh, sht, ut, sfac,
     kmat, emat, slopes,
     colbuf, rowbuf1, rowbuf2, csc, rb, tb,
@@ -41,8 +41,18 @@
     q = h * 2 + c
     y = h * 4 + l
 
-    def rows_dev(d):
-        return (lax.rem(me + d, 32), mp)
+    drains = []
+
+    def drain(first, count, copy):
+        def wait(i, carry):
+            copy(i).wait_send()
+            return carry
+        drains.append((first, count, wait))
+
+    def flush():
+        for first, count, wait in drains:
+            lax.fori_loop(first, count, wait, 0)
+        drains.clear()
 
     def z_dev(d):
         return (lax.rem(z + d, 8) * 4 + q, mp)
@@ -55,23 +65,32 @@
         other = lax.rem(y + d, 8)
         return (z * 4 + (other // 4) * 2 + c, x * 4 + lax.rem(other, 4))
 
+    core_dev = (z * 4 + h * 2 + (1 - c), mp)
+    y4_dev = (z * 4 + (1 - h) * 2 + c, mp)
+    diag_dev = (z * 4 + (1 - h) * 2 + (1 - c), mp)
+
     barrier = pltpu.get_barrier_semaphore()
-
-    def greet(group, count):
-        def body(d, carry):
+    pl.semaphore_signal(barrier, inc=1, device_id=diag_dev, device_id_type=MESH)
+
+    def greet(d, carry):
+        for group in (z_dev, y_dev, cx_dev):
             pl.semaphore_signal(barrier, inc=1, device_id=group(d), device_id_type=MESH)
-            return carry
-        lax.fori_loop(1, count, body, 0)
-
-    greet(rows_dev, 32)
-    greet(cx_dev, 8)
-    greet(y_dev, 8)
-
+        return carry
+
+    lax.fori_loop(1, 8, greet, 0)
+
+    load_p = pltpu.make_async_copy(pr_hbm, pr_ref, local_sem.at[2])
+    load_p.start()
+    load_pos = pltpu.make_async_copy(pos_hbm, pos_ref, local_sem.at[3])
+    load_pos.start()
+    load_scale = pltpu.make_async_copy(scale_hbm, scale_ref, local_sem.at[4])
+    load_scale.start()
     load_t = pltpu.make_async_copy(tp_hbm, tp, local_sem.at[0])
     load_t.start()
     load_s = pltpu.make_async_copy(sp_hbm, sp, local_sem.at[1])
     load_s.start()
 
+    load_p.wait()
     wide = pr_ref[...].astype(F32)
     for other in range(4):
         first = wide[:, other * 1024 : other * 1024 + 512]
@@ -79,17 +98,33 @@
         send_p[other] = jnp.concatenate([first, second], axis=0).astype(BF16)
     pg[pl.ds(me, 1)] = send_p[pl.ds(q, 1)]
 
-    pl.semaphore_wait(barrier, 45)
-
-    def send_proto(d, carry):
-        target = lax.rem(me + d, 32)
-        pltpu.make_async_remote_copy(
-            send_p.at[lax.rem(target, 4)], pg.at[me], pg_send.at[d], pg_recv.at[d],
-            device_id=(target, mp), device_id_type=MESH,
-        ).start()
-        return carry
-
-    lax.fori_loop(1, 32, send_proto, 0)
+    pl.semaphore_wait(barrier, 22)
+
+    def relative(j):
+        return (h + (j // 2)) % 2 * 2 + (c + j % 2) % 2
+
+    def quad_copy(j, target):
+        return pltpu.make_async_remote_copy(
+            send_p.at[relative(j)], pg.at[me], pg_send.at[j], pg_recv.at[j],
+            device_id=target, device_id_type=MESH,
+        )
+
+    quad_copies = [quad_copy(2, y4_dev), quad_copy(3, diag_dev), quad_copy(1, core_dev)]
+
+    def ring_copy(j, d):
+        at = z * 4 + relative(j)
+        return pltpu.make_async_remote_copy(
+            pg.at[at], pg.at[at], pg_send.at[d * 4 + j], pg_recv.at[d * 4 + j],
+            device_id=z_dev(d), device_id_type=MESH,
+        )
+
+    def ring_start(j):
+        for d in (4, 5, 3, 6, 2, 7, 1):
+            ring_copy(j, d).start()
+
+    for copy in quad_copies:
+        copy.start()
+    ring_start(0)
 
     def pick(patches, m):
         parts = []
@@ -99,8 +134,6 @@
             parts.append(dot(hot, patches[m, image], 0, 0))
         return jnp.concatenate(parts, axis=0).astype(BF16)
 
-    core_dev = (z * 4 + h * 2 + (1 - c), mp)
-    y4_dev = (z * 4 + (1 - h) * 2 + c, mp)
     q_far = (1 - h) * 2 + c
     mine = pl.ds(pl.multiple_of(x * 32, 32), 32)
 
@@ -122,11 +155,14 @@
             device_id=core_dev, device_id_type=MESH,
         )
 
+    load_pos.wait()
     load_t.wait()
     for m in range(2):
         tx[m, pl.ds(q, 1)] = pick(tp, m)[None]
     y4_copy(tx, tx_send, tx_recv).start()
     core_copy(tx, tx_send, tx_recv).start()
+    quad_copies[2].wait_recv()
+    ring_start(1)
     load_s.wait()
     for m in range(2):
         sx[m, pl.ds(q, 1)] = pick(sp, m)[None]
@@ -141,6 +177,9 @@
             return carry
 
         lax.fori_loop(1, 8, body, 0)
+        drain(8, 9, lambda i: y4_copy(buf, send, recv))
+        drain(0, 1, lambda i: core_copy(buf, send, recv))
+        drain(1, 8, lambda i: far_copy(buf, send, recv, i))
 
     def rows_arrive(buf, send, recv):
         core_copy(buf, send, recv).wait_recv()
@@ -151,16 +190,10 @@
 
         lax.fori_loop(1, 8, body, 0)
 
-    def rows_sent(buf, send, recv):
-        y4_copy(buf, send, recv).wait_send()
-        core_copy(buf, send, recv).wait_send()
-
-        def body(i, carry):
-            far_copy(buf, send, recv, i).wait_send()
-            return carry
-
-        lax.fori_loop(1, 8, body, 0)
-
+    quad_copies[0].wait_recv()
+    ring_start(2)
+    quad_copies[1].wait_recv()
+    ring_start(3)
     forward_far(tx, tx_send, tx_recv)
     forward_far(sx, sx_send, sx_recv)
 
@@ -170,6 +203,87 @@
             values = tx[m, part].astype(F32)
             factor = lax.rsqrt(jnp.sum(values * values, axis=1, keepdims=True) + EPSILON)
             th[m, part * 128 : part * 128 + 128, :] = (values * factor).astype(BF16)
+
+    def ring_wait(d, carry):
+        for j in range(4):
+            ring_copy(j, d).wait_recv()
+        return carry
+
+    lax.fori_loop(1, 8, ring_wait, 0)
+
+    def unpack(b, total):
+        block = pg[b].astype(F32)
+        rows = jnp.concatenate([block[0:8, :], block[8:16, :]], axis=1)
+        pu[pl.ds(pl.multiple_of(b * 8, 8), 8), :] = rows
+        return total + rows * rows
+
+    total = lax.fori_loop(0, 32, unpack, jnp.zeros((8, 1024), F32))
+    pfac[...] = jnp.broadcast_to(
+        lax.rsqrt(jnp.sum(total, axis=0, keepdims=True) + EPSILON), (8, 1024)
+    )
+
+    def normalize(b, carry):
+        at = pl.ds(pl.multiple_of(b * 16, 16), 16)
+        unit = pu[at, :] * pfac[0:1, :]
+        pu[at, :] = unit
+        ph[at, :] = unit.astype(BF16)
+        return carry
+
+    lax.fori_loop(0, 16, normalize, 0)
+
+    def tile_send(buf, send, recv, group):
+        def body(d, carry):
+            pltpu.make_async_remote_copy(
+                buf.at[0], buf.at[d], send.at[d], recv.at[d], device_id=group(d), device_id_type=MESH
+            ).start()
+            return carry
+        lax.fori_loop(1, 8, body, 0)
+        drain(1, 8, lambda d: pltpu.make_async_remote_copy(
+            buf.at[0], buf.at[d], send.at[d], recv.at[d], device_id=group(d), device_id_type=MESH
+        ))
+
+    def tile_recv(buf, send, recv, group):
+        def body(d, carry):
+            pltpu.make_async_remote_copy(
+                buf.at[0], buf.at[d], send.at[d], recv.at[d], device_id=group(d), device_id_type=MESH
+            ).wait_recv()
+            return carry
+        lax.fori_loop(1, 8, body, 0)
+        return jnp.sum(buf[...], axis=0)
+
+    def col_store(it, m, tile, sums):
+        width = sums.shape[1] // 128
+        for part in range(width):
+            row = tile * width + part
+            colbuf[it, m, 0, row : row + 1, :] = sums[:, part * 128 : part * 128 + 128]
+
+    def lane_sums(block):
+        return jnp.sum(block.T, axis=0, keepdims=True)
+
+    def spread(row):
+        return jnp.broadcast_to(row, (128, 128)).T
+
+    def col_send_start(it, m):
+        tile_send(colbuf.at[it, m], col_send.at[it, m], col_recv.at[it, m], z_dev)
+
+    for m in range(2):
+        for tile in range(4):
+            at = slice(tile * 256, tile * 256 + 256)
+            scores = dot(th[m], ph[:, at], 1, 0)
+            values = jnp.exp2(scores * TEACHER_EXP2)
+            kmat[m, :, at] = values
+            col_store(0, m, tile, jnp.sum(values, axis=0, keepdims=True))
+        col_send_start(0, m)
+
+    for copy in quad_copies:
+        copy.wait_send()
+
+    def ring_sent(d, carry):
+        for j in range(4):
+            ring_copy(j, d).wait_send()
+        return carry
+
+    lax.fori_loop(1, 8, ring_sent, 0)
 
     rows_arrive(sx, sx_send, sx_recv)
     for m in range(2):
@@ -184,76 +298,6 @@
             sfac[m, part] = jnp.broadcast_to(factor, (8, 128))
             sh[m, at, :] = jnp.concatenate([unit[:128, :].T, unit[128:, :].T], axis=1).astype(BF16)
 
-    def wait_proto(d, carry):
-        pltpu.make_async_remote_copy(
-            send_p.at[0], pg.at[me], pg_send.at[d], pg_recv.at[d],
-            device_id=rows_dev(d), device_id_type=MESH,
-        ).wait_recv()
-        return carry
-
-    lax.fori_loop(1, 32, wait_proto, 0)
-
-    def unpack(b, total):
-        block = pg[b].astype(F32)
-        rows = jnp.concatenate([block[0:8, :], block[8:16, :]], axis=1)
-        pu[pl.ds(pl.multiple_of(b * 8, 8), 8), :] = rows
-        return total + rows * rows
-
-    total = lax.fori_loop(0, 32, unpack, jnp.zeros((8, 1024), F32))
-    pfac[...] = jnp.broadcast_to(
-        lax.rsqrt(jnp.sum(total, axis=0, keepdims=True) + EPSILON), (8, 1024)
-    )
-
-    def normalize(b, carry):
-        at = pl.ds(pl.multiple_of(b * 16, 16), 16)
-        unit = pu[at, :] * pfac[0:1, :]
-        pu[at, :] = unit
-        ph[at, :] = unit.astype(BF16)
-        return carry
-
-    lax.fori_loop(0, 16, normalize, 0)
-
-    def tile_send(buf, send, recv, group):
-        def body(d, carry):
-            pltpu.make_async_remote_copy(
-                buf.at[0], buf.at[d], send.at[d], recv.at[d], device_id=group(d), device_id_type=MESH
-            ).start()
-            return carry
-        lax.fori_loop(1, 8, body, 0)
-
-    def tile_recv(buf, send, recv, group):
-        def body(d, carry):
-            pltpu.make_async_remote_copy(
-                buf.at[0], buf.at[d], send.at[d], recv.at[d], device_id=group(d), device_id_type=MESH
-            ).wait_recv()
-            return carry
-        lax.fori_loop(1, 8, body, 0)
-        return jnp.sum(buf[...], axis=0)
-
-    def col_store(it, m, tile, sums):
-        width = sums.shape[1] // 128
-        for part in range(width):
-            row = tile * width + part
-            colbuf[it, m, 0, row : row + 1, :] = sums[:, part * 128 : part * 128 + 128]
-
-    def lane_sums(block):
-        return jnp.sum(block.T, axis=0, keepdims=True)
-
-    def spread(row):
-        return jnp.broadcast_to(row, (128, 128)).T
-
-    def col_send_start(it, m):
-        tile_send(colbuf.at[it, m], col_send.at[it, m], col_recv.at[it, m], z_dev)
-
-    for m in range(2):
-        for tile in range(4):
-            at = slice(tile * 256, tile * 256 + 256)
-            scores = dot(th[m], ph[:, at], 1, 0)
-            values = jnp.exp2(scores * TEACHER_EXP2)
-            kmat[m, :, at] = values
-            col_store(0, m, tile, jnp.sum(values, axis=0, keepdims=True))
-        col_send_start(0, m)
-
     for m in range(2):
         acc = None
         for tile in range(4):
@@ -266,6 +310,7 @@
         for part in range(4):
             rowbuf1[0, m, 0, 4 + part : 5 + part, :] = lane_sums(acc[part * 128 : part * 128 + 128, :])
 
+    load_scale.wait()
     loss_factor = scale_ref[0] * (1.0 / (2 * 4096 * 0.1))
 
     for it in range(ITERS):
@@ -281,6 +326,7 @@
             if it > 0:
                 rowbuf1[it, m, 0, 4:8, :] = jnp.zeros((4, 128), F32)
             tile_send(rowbuf1.at[it, m], row1_send.at[it, m], row1_recv.at[it, m], cx_dev)
+        flush()
         for m in range(2):
             total = tile_recv(rowbuf1.at[it, m], row1_send.at[it, m], row1_recv.at[it, m], cx_dev)
             rowbuf2[it, m, 0] = total
@@ -327,7 +373,14 @@
         ).start()
         return carry
 
+    def rr_copy(d):
+        return pltpu.make_async_remote_copy(
+            send_r.at[d], rr.at[me], rr_send.at[d], rr_recv.at[d],
+            device_id=(lax.rem(me + d, 32), mp), device_id_type=MESH,
+        )
+
     lax.fori_loop(1, 32, send_back, 0)
+    drain(1, 32, rr_copy)
     own = pterm[pl.ds(pl.multiple_of(me * 8, 8), 8), :]
     rr[pl.ds(me, 1)] = jnp.concatenate([own[:, :512], own[:, 512:]], axis=0).astype(BF16)[None]
 
@@ -359,6 +412,7 @@
         return carry
 
     lax.fori_loop(1, 8, fs_start, 0)
+    drain(1, 8, fs_copy)
     fr[pl.ds(0, 1)] = fs[pl.ds(x * 2 + c, 1)]
     lax.fori_loop(1, 8, fs_wait, 0)
 
@@ -389,18 +443,13 @@
         return carry
 
     lax.fori_loop(1, 8, gr_start, 0)
+    drain(1, 8, gr_copy)
     grecv[pl.ds(0, 1)] = gsend[pl.ds(y, 1)]
     lax.fori_loop(1, 8, gr_wait, 0)
     total = jnp.sum(grecv[...].astype(F32), axis=0)
     for m in range(2):
-        gs_ref[:, m * 128 : m * 128 + 128] = (
+        gs_ref[m] = (
             total[:, m * 128 : m * 128 + 128] * sfac[m, pl.ds(q, 1)][0, 0:1, :]
-        )
-
-    def rr_copy(d):
-        return pltpu.make_async_remote_copy(
-            send_r.at[d], rr.at[me], rr_send.at[d], rr_recv.at[d],
-            device_id=rows_dev(d), device_id_type=MESH,
         )
 
     def rr_wait(d, carry):
@@ -415,58 +464,27 @@
         gp_ref[:, part * 1024 : part * 1024 + 512] = total[0:8, :]
         gp_ref[:, part * 1024 + 512 : part * 1024 + 1024] = total[8:16, :]
 
-    rows_sent(tx, tx_send, tx_recv)
-    rows_sent(sx, sx_send, sx_recv)
-
-    def drain31(d, carry):
-        pltpu.make_async_remote_copy(
-            send_p.at[0], pg.at[me], pg_send.at[d], pg_recv.at[d],
-            device_id=rows_dev(d), device_id_type=MESH,
-        ).wait_send()
-        rr_copy(d).wait_send()
-        return carry
-
-    lax.fori_loop(1, 32, drain31, 0)
-
-    def drain7(d, carry):
-        fs_copy(d).wait_send()
-        gr_copy(d).wait_send()
-        for it in range(ITERS):
-            for m in range(2):
-                for buf, send, recv, group in (
-                    (colbuf, col_send, col_recv, z_dev),
-                    (rowbuf1, row1_send, row1_recv, cx_dev),
-                    (rowbuf2, row2_send, row2_recv, y_dev),
-                ):
-                    pltpu.make_async_remote_copy(
-                        buf.at[it, m, 0], buf.at[it, m, d], send.at[it, m, d], recv.at[it, m, d],
-                        device_id=group(d), device_id_type=MESH,
-                    ).wait_send()
-        return carry
-
-    lax.fori_loop(1, 8, drain7, 0)
+    flush()
 
 
 def local(student_patches, teacher_patches, positions, prototypes, loss_scale):
     vmem = pl.BlockSpec(memory_space=pltpu.VMEM)
+    hbm = pl.BlockSpec(memory_space=pltpu.HBM)
     dma = pltpu.SemaphoreType.DMA
     grad_t, grad_protos = pl.pallas_call(
         kernel,
         out_shape=(
-            jax.ShapeDtypeStruct((16, 256), F32),
+            jax.ShapeDtypeStruct((2, 16, 128), F32),
             jax.ShapeDtypeStruct((8, 4096), F32),
         ),
-        in_specs=[
-            pl.BlockSpec(memory_space=pl.ANY),
-            pl.BlockSpec(memory_space=pl.ANY),
-            vmem,
-            vmem,
-            pl.BlockSpec(memory_space=pltpu.SMEM),
-        ],
+        in_specs=[hbm] * 5,
         out_specs=(vmem, vmem),
         scratch_shapes=[
             pltpu.VMEM((2, 2, 256, 256), BF16),
             pltpu.VMEM((2, 2, 256, 256), BF16),
+            pltpu.VMEM((2, 2, 64), jnp.int32),
+            pltpu.VMEM((8, 4096), BF16),
+            pltpu.SMEM((1,), F32),
             pltpu.VMEM((4, 16, 512), BF16),
             pltpu.VMEM((32, 16, 512), BF16),
             pltpu.VMEM((256, 1024), F32),
@@ -495,7 +513,7 @@
             pltpu.VMEM((8, 64, 512), BF16),
             pltpu.VMEM((8, 16, 256), BF16),
             pltpu.VMEM((8, 16, 256), BF16),
-            dma((2,)),
+            dma((5,)),
             dma((32,)),
             dma((32,)),
             dma((9,)),
@@ -516,15 +534,14 @@
             dma((8,)),
         ],
         compiler_params=pltpu.CompilerParams(
-            collective_id=0, has_side_effects=True, vmem_limit_bytes=48 * 2**20
+            collective_id=0, has_side_effects=True, vmem_limit_bytes=60 * 2**20
         ),
         cost_estimate=pl.CostEstimate(
             flops=2_200_000_000, bytes_accessed=2_000_000, transcendentals=2_000_000
         ),
         name="ibot_head",
     )(student_patches, teacher_patches, positions, prototypes, loss_scale)
-    grad_student = jnp.transpose(grad_t.reshape(16, 2, 128), (1, 2, 0))
-    return grad_student, grad_protos
+    return jnp.transpose(grad_t, (0, 2, 1)), grad_protos
 
 
 def solution(mesh):

time: 115 us -> 98.7 us (0.86)
  Pallas kernels: 109 us -> 94.3 us
  local copies, waits for them, and re-layouts: 4.86 us -> 2.89 us
    pallas_call x1, Pallas kernels: 109 us -> 94.3 us  [local(): pl.pallas_call(kernel, out_shape=(jax.ShapeDtypeStruct((2, 16, 128), F32)...]
    unnamed x9 -> x2, local copies, waits for them, and re-layouts: 4.25 us -> 2.89 us
where the time goes in v2:
time: 98.7 us; the launch traced here: 98.4 us
  Pallas kernels  94.3 us (96%)
  local copies, waits for them, and re-layouts  2.89 us (3%)
  between operations  1.29 us (1%)
    pallas_call x1, Pallas kernels, local(): pl.pallas_call(kernel, out_shape=(jax.ShapeDtypeStruct((2, 16, 128), F32)...  94.3 us
    unnamed x2, local copies, waits for them, and re-layouts  2.89 us

profile of v2, /device:TPU:1, one launch (start us, length us, event | category | flops | bytes accessed | tf_op | source)
XLA Modules:
  0.0 98.4 jit_solution(11234809902021471480)
XLA Ops:
  1.3 94.3 %ibot_head.1 = (f32[2,16,128]{2,1,0:T(8,128)}, f32[8,4096]{1,0:T(8,128)}) custom-call(bf16[2,2,256,256]{3,2,1,0:T(8,128)(2,1)} %sp_hbm.1, bf16[2,2,256,256]{3,2,1,0:T(8,128)(2,1)} %tp_hbm.1, s32[2,2,64]{2,1,0:T(2,128)} %pos_hbm.1, bf16[8,4096]{1,0:T(8,128)(2,1)} %pr_hbm.1, f32[1]{0:T(128)S(6)} %copy.9.scale_hbm), custom_call_target="tpu_custom_call" | custom-call | flops 2200000000 | bytes 2000000 | tf_op jit(solution)/shard_map/ibot_head/pallas_call | solution.py:474
  95.5 1.3 %copy.10 = f32[2,128,16]{1,2,0:T(8,128)} copy(f32[2,128,16]{1,2,0:T(8,128)} %bitcast.1) | data formatting | bytes 32768
  96.9 1.6 %copy.11 = f32[8,4096]{1,0:T(8,128)} copy(f32[8,4096]{1,0:T(8,128)} %get-tuple-element.9) | data formatting | bytes 262144

commit v3 on v2

--- a/solution.py
+++ b/solution.py
@@ -204,20 +204,24 @@
             factor = lax.rsqrt(jnp.sum(values * values, axis=1, keepdims=True) + EPSILON)
             th[m, part * 128 : part * 128 + 128, :] = (values * factor).astype(BF16)
 
-    def ring_wait(d, carry):
-        for j in range(4):
-            ring_copy(j, d).wait_recv()
-        return carry
+    def ring_wait(d, first):
+        for j in range(2):
+            ring_copy(first + j, d).wait_recv()
+        return first
+
+    def unpack_half(half):
+        def unpack(i, total):
+            b = i // 2 * 4 + half * 2 + lax.rem(i, 2)
+            block = pg[b].astype(F32)
+            rows = jnp.concatenate([block[0:8, :], block[8:16, :]], axis=1)
+            pu[pl.ds(pl.multiple_of(b * 8, 8), 8), :] = rows
+            return total + rows * rows
+        return unpack
 
     lax.fori_loop(1, 8, ring_wait, 0)
-
-    def unpack(b, total):
-        block = pg[b].astype(F32)
-        rows = jnp.concatenate([block[0:8, :], block[8:16, :]], axis=1)
-        pu[pl.ds(pl.multiple_of(b * 8, 8), 8), :] = rows
-        return total + rows * rows
-
-    total = lax.fori_loop(0, 32, unpack, jnp.zeros((8, 1024), F32))
+    total = lax.fori_loop(0, 16, unpack_half(h), jnp.zeros((8, 1024), F32))
+    lax.fori_loop(1, 8, ring_wait, 2)
+    total = lax.fori_loop(0, 16, unpack_half(1 - h), total)
     pfac[...] = jnp.broadcast_to(
         lax.rsqrt(jnp.sum(total, axis=0, keepdims=True) + EPSILON), (8, 1024)
     )
@@ -231,25 +235,27 @@
 
     lax.fori_loop(0, 16, normalize, 0)
 
+    ring_order = (4, 5, 3, 6, 2, 7, 1)
+    cx_order = (4, 5, 2, 3, 6, 7, 1)
+
+    def tile_copy(buf, send, recv, device, d):
+        return pltpu.make_async_remote_copy(
+            buf.at[0], buf.at[d], send.at[d], recv, device_id=device, device_id_type=MESH
+        )
+
     def tile_send(buf, send, recv, group):
-        def body(d, carry):
-            pltpu.make_async_remote_copy(
-                buf.at[0], buf.at[d], send.at[d], recv.at[d], device_id=group(d), device_id_type=MESH
-            ).start()
-            return carry
-        lax.fori_loop(1, 8, body, 0)
-        drain(1, 8, lambda d: pltpu.make_async_remote_copy(
-            buf.at[0], buf.at[d], send.at[d], recv.at[d], device_id=group(d), device_id_type=MESH
-        ))
-
-    def tile_recv(buf, send, recv, group):
-        def body(d, carry):
-            pltpu.make_async_remote_copy(
-                buf.at[0], buf.at[d], send.at[d], recv.at[d], device_id=group(d), device_id_type=MESH
-            ).wait_recv()
-            return carry
-        lax.fori_loop(1, 8, body, 0)
+        devices, order = group
+        for d in order:
+            tile_copy(buf, send, recv, devices[d], d).start()
+        drain(1, 8, lambda d: tile_copy(buf, send, recv, core_dev, d))
+
+    def tile_recv(buf, recv):
+        pltpu.make_async_copy(buf.at[pl.ds(1, 7)], buf.at[pl.ds(1, 7)], recv).wait()
         return jnp.sum(buf[...], axis=0)
+
+    z_group = ([z_dev(d) for d in range(8)], ring_order)
+    y_group = ([y_dev(d) for d in range(8)], ring_order)
+    cx_group = ([cx_dev(d) for d in range(8)], cx_order)
 
     def col_store(it, m, tile, sums):
         width = sums.shape[1] // 128
@@ -264,7 +270,7 @@
         return jnp.broadcast_to(row, (128, 128)).T
 
     def col_send_start(it, m):
-        tile_send(colbuf.at[it, m], col_send.at[it, m], col_recv.at[it, m], z_dev)
+        tile_send(colbuf.at[it, m], col_send.at[it, m], col_recv.at[it, m], z_group)
 
     for m in range(2):
         for tile in range(4):
@@ -315,7 +321,7 @@
 
     for it in range(ITERS):
         for m in range(2):
-            total = tile_recv(colbuf.at[it, m], col_send.at[it, m], col_recv.at[it, m], z_dev)
+            total = tile_recv(colbuf.at[it, m], col_recv.at[it, m])
             csc[m] = 1.0 / total
             for part in range(4):
                 at = slice(part * 128, part * 128 + 128)
@@ -325,14 +331,24 @@
                 rowbuf1[it, m, 0, part : part + 1, :] = lane_sums(acc)
             if it > 0:
                 rowbuf1[it, m, 0, 4:8, :] = jnp.zeros((4, 128), F32)
-            tile_send(rowbuf1.at[it, m], row1_send.at[it, m], row1_recv.at[it, m], cx_dev)
+            tile_send(rowbuf1.at[it, m], row1_send.at[it, m], row1_recv.at[it, m], cx_group)
         flush()
+        if it == 1:
+            for m in range(2):
+                for tile in range(8):
+                    at = slice(tile * 128, tile * 128 + 128)
+                    emat[m, :, at] = emat[m, :, at] * tb[m]
+        if it == ITERS - 1:
+            for m in range(2):
+                for tile in range(8):
+                    at = slice(tile * 128, tile * 128 + 128)
+                    kmat[m, :, at] = kmat[m, :, at] * csc[m, tile : tile + 1, :]
         for m in range(2):
-            total = tile_recv(rowbuf1.at[it, m], row1_send.at[it, m], row1_recv.at[it, m], cx_dev)
+            total = tile_recv(rowbuf1.at[it, m], row1_recv.at[it, m])
             rowbuf2[it, m, 0] = total
-            tile_send(rowbuf2.at[it, m], row2_send.at[it, m], row2_recv.at[it, m], y_dev)
+            tile_send(rowbuf2.at[it, m], row2_send.at[it, m], row2_recv.at[it, m], y_group)
         for m in range(2):
-            total = tile_recv(rowbuf2.at[it, m], row2_send.at[it, m], row2_recv.at[it, m], y_dev)
+            total = tile_recv(rowbuf2.at[it, m], row2_recv.at[it, m])
             inverse = 1.0 / total[0:4, :]
             if it == ITERS - 1:
                 inverse = inverse * loss_factor
@@ -352,8 +368,7 @@
     for m in range(2):
         for tile in range(8):
             at = slice(tile * 128, tile * 128 + 128)
-            target = kmat[m, :, at] * rb[m] * csc[m, tile : tile + 1, :]
-            slopes[m, :, at] = (emat[m, :, at] * tb[m] - target).astype(BF16)
+            slopes[m, :, at] = (emat[m, :, at] - kmat[m, :, at] * rb[m]).astype(BF16)
 
     for tile in range(4):
         at = slice(tile * 256, tile * 256 + 256)
@@ -373,14 +388,28 @@
         ).start()
         return carry
 
-    def rr_copy(d):
-        return pltpu.make_async_remote_copy(
-            send_r.at[d], rr.at[me], rr_send.at[d], rr_recv.at[d],
-            device_id=(lax.rem(me + d, 32), mp), device_id_type=MESH,
-        )
-
-    lax.fori_loop(1, 32, send_back, 0)
-    drain(1, 32, rr_copy)
+    def back_to(i):
+        step = i // 4
+        dz = lax.rem(4 + (step + 1) // 2 * (2 * lax.rem(step, 2) - 1), 8)
+        j = 3 - lax.rem(i, 4)
+        q_to = lax.rem(h + j // 2, 2) * 2 + lax.rem(c + lax.rem(j, 2), 2)
+        return lax.rem(z + dz, 8) * 4 + q_to
+
+    def rr_copy(i):
+        return pltpu.make_async_remote_copy(
+            send_r.at[i], rr.at[me], rr_send.at[i], rr_recv.at[i],
+            device_id=(back_to(i), mp), device_id_type=MESH,
+        )
+
+    def send_back(i, carry):
+        rows = pterm[pl.ds(pl.multiple_of(back_to(i) * 8, 8), 8), :]
+        packed = jnp.concatenate([rows[:, :512], rows[:, 512:]], axis=0)
+        send_r[pl.ds(i, 1)] = packed.astype(BF16)[None]
+        rr_copy(i).start()
+        return carry
+
+    lax.fori_loop(0, 31, send_back, 0)
+    drain(0, 31, rr_copy)
     own = pterm[pl.ds(pl.multiple_of(me * 8, 8), 8), :]
     rr[pl.ds(me, 1)] = jnp.concatenate([own[:, :512], own[:, 512:]], axis=0).astype(BF16)[None]
 
@@ -456,7 +485,8 @@
         rr_copy(d).wait_recv()
         return carry
 
-    lax.fori_loop(1, 32, rr_wait, 0)
+    flush()
+    lax.fori_loop(0, 31, rr_wait, 0)
     for part in range(4):
         total = rr[part].astype(F32)
         for zz in range(1, 8):
@@ -474,8 +504,8 @@
     grad_t, grad_protos = pl.pallas_call(
         kernel,
         out_shape=(
-            jax.ShapeDtypeStruct((2, 16, 128), F32),
-            jax.ShapeDtypeStruct((8, 4096), F32),
+            pltpu.VMEM((2, 16, 128), F32),
+            pltpu.VMEM((8, 4096), F32),
         ),
         in_specs=[hbm] * 5,
         out_specs=(vmem, vmem),
@@ -521,11 +551,11 @@
             dma((9,)),
             dma((9,)),
             dma((ITERS, 2, 8)),
+            dma((ITERS, 2)),
             dma((ITERS, 2, 8)),
+            dma((ITERS, 2)),
             dma((ITERS, 2, 8)),
-            dma((ITERS, 2, 8)),
-            dma((ITERS, 2, 8)),
-            dma((ITERS, 2, 8)),
+            dma((ITERS, 2)),
             dma((32,)),
             dma((32,)),
             dma((8,)),

time: 98.7 us -> 92.2 us (0.934)
  Pallas kernels: 94.3 us -> 89.5 us
  local copies, waits for them, and re-layouts: 2.89 us -> 1.26 us
    pallas_call x1, Pallas kernels: 94.3 us -> 89.5 us  [local(): pl.pallas_call(kernel, out_shape=(pltpu.VMEM((2, 16, 128), F32), pltpu.VM...]
    unnamed x2, local copies, waits for them, and re-layouts: 2.89 us -> 1.26 us
where the time goes in v3:
time: 92.2 us; the launch traced here: 92 us
  Pallas kernels  89.5 us (97%)
  between operations  1.29 us (1%)
  local copies, waits for them, and re-layouts  1.26 us (1%)
    pallas_call x1, Pallas kernels, local(): pl.pallas_call(kernel, out_shape=(pltpu.VMEM((2, 16, 128), F32), pltpu.VM...  89.5 us

profile of v3, /device:TPU:1, one launch (start us, length us, event | category | flops | bytes accessed | tf_op | source)
XLA Modules:
  0.0 92.0 jit_solution(1085746758548144725)
XLA Ops:
  1.3 89.5 %ibot_head.1 = (f32[2,16,128]{2,1,0:T(8,128)S(1)}, f32[8,4096]{1,0:T(8,128)S(1)}) custom-call(bf16[2,2,256,256]{3,2,1,0:T(8,128)(2,1)} %sp_hbm.1, bf16[2,2,256,256]{3,2,1,0:T(8,128)(2,1)} %tp_hbm.1, s32[2,2,64]{2,1,0:T(2,128)} %pos_hbm.1, bf16[8,4096]{1,0:T(8,128)(2,1)} %pr_hbm.1, f32[1]{0:T(128)S(6)} %copy.11.scale_hbm), custom_call_target="tpu_custom_call" | custom-call | flops 2200000000 | bytes 2000000 | tf_op jit(solution)/shard_map/ibot_head/pallas_call | solution.py:504
  90.8 0.6 copy.9
  91.4 0.7 copy.10

commit v4 on v3

--- a/solution.py
+++ b/solution.py
@@ -22,14 +22,14 @@
 
 
 def kernel(
-    sp_hbm, tp_hbm, pos_hbm, pr_hbm, scale_hbm,
+    sp_hbm, tp_hbm, pos_hbm, pr_hbm,
     gs_ref, gp_ref,
-    sp, tp, pos_ref, pr_ref, scale_ref, send_p, pg, pu, ph, pfac,
+    sp, tp, pos_ref, pr_ref, send_p, pg, pu, ph, pfac,
     tx, sx, th, sh, sht, ut, sfac,
     kmat, emat, slopes,
     colbuf, rowbuf1, rowbuf2, csc, rb, tb,
     send_r, rr, pterm, fs, fr, gsend, grecv,
-    local_sem, pg_send, pg_recv,
+    local_sem, pg_send, pg_recv, ring_recv,
     tx_send, tx_recv, sx_send, sx_recv,
     col_send, col_recv, row1_send, row1_recv, row2_send, row2_recv,
     rr_send, rr_recv, fr_send, fr_recv, gr_send, gr_recv,
@@ -41,18 +41,8 @@
     q = h * 2 + c
     y = h * 4 + l
 
-    drains = []
-
-    def drain(first, count, copy):
-        def wait(i, carry):
-            copy(i).wait_send()
-            return carry
-        drains.append((first, count, wait))
-
-    def flush():
-        for first, count, wait in drains:
-            lax.fori_loop(first, count, wait, 0)
-        drains.clear()
+    def take(ref, sem):
+        pltpu.make_async_copy(ref, ref, sem).wait()
 
     def z_dev(d):
         return (lax.rem(z + d, 8) * 4 + q, mp)
@@ -83,8 +73,6 @@
     load_p.start()
     load_pos = pltpu.make_async_copy(pos_hbm, pos_ref, local_sem.at[3])
     load_pos.start()
-    load_scale = pltpu.make_async_copy(scale_hbm, scale_ref, local_sem.at[4])
-    load_scale.start()
     load_t = pltpu.make_async_copy(tp_hbm, tp, local_sem.at[0])
     load_t.start()
     load_s = pltpu.make_async_copy(sp_hbm, sp, local_sem.at[1])
@@ -105,7 +93,7 @@
 
     def quad_copy(j, target):
         return pltpu.make_async_remote_copy(
-            send_p.at[relative(j)], pg.at[me], pg_send.at[j], pg_recv.at[j],
+            send_p.at[relative(j)], pg.at[me], pg_send, pg_recv.at[j],
             device_id=target, device_id_type=MESH,
         )
 
@@ -114,7 +102,7 @@
     def ring_copy(j, d):
         at = z * 4 + relative(j)
         return pltpu.make_async_remote_copy(
-            pg.at[at], pg.at[at], pg_send.at[d * 4 + j], pg_recv.at[d * 4 + j],
+            pg.at[at], pg.at[at], pg_send, ring_recv.at[j // 2],
             device_id=z_dev(d), device_id_type=MESH,
         )
 
@@ -139,19 +127,19 @@
 
     def far_copy(buf, send, recv, i):
         return pltpu.make_async_remote_copy(
-            buf.at[:, q_far, mine], buf.at[:, q_far, mine], send.at[i], recv.at[i],
+            buf.at[:, q_far, mine], buf.at[:, q_far, mine], send, recv.at[2],
             device_id=cx_dev(i), device_id_type=MESH,
         )
 
     def y4_copy(buf, send, recv):
         return pltpu.make_async_remote_copy(
-            buf.at[:, q, mine], buf.at[:, q, mine], send.at[8], recv.at[8],
+            buf.at[:, q, mine], buf.at[:, q, mine], send, recv.at[1],
             device_id=y4_dev, device_id_type=MESH,
         )
 
     def core_copy(buf, send, recv):
         return pltpu.make_async_remote_copy(
-            buf.at[:, q], buf.at[:, q], send.at[0], recv.at[0],
+            buf.at[:, q], buf.at[:, q], send, recv.at[0],
             device_id=core_dev, device_id_type=MESH,
         )
 
@@ -177,18 +165,10 @@
             return carry
 
         lax.fori_loop(1, 8, body, 0)
-        drain(8, 9, lambda i: y4_copy(buf, send, recv))
-        drain(0, 1, lambda i: core_copy(buf, send, recv))
-        drain(1, 8, lambda i: far_copy(buf, send, recv, i))
 
     def rows_arrive(buf, send, recv):
         core_copy(buf, send, recv).wait_recv()
-
-        def body(i, carry):
-            far_copy(buf, send, recv, i).wait_recv()
-            return carry
-
-        lax.fori_loop(1, 8, body, 0)
+        take(buf.at[:, pl.ds(0, 2), pl.ds(0, 112)], recv.at[2])
 
     quad_copies[0].wait_recv()
     ring_start(2)
@@ -203,11 +183,6 @@
             values = tx[m, part].astype(F32)
             factor = lax.rsqrt(jnp.sum(values * values, axis=1, keepdims=True) + EPSILON)
             th[m, part * 128 : part * 128 + 128, :] = (values * factor).astype(BF16)
-
-    def ring_wait(d, first):
-        for j in range(2):
-            ring_copy(first + j, d).wait_recv()
-        return first
 
     def unpack_half(half):
         def unpack(i, total):
@@ -218,9 +193,9 @@
             return total + rows * rows
         return unpack
 
-    lax.fori_loop(1, 8, ring_wait, 0)
+    take(pg.at[pl.ds(0, 14)], ring_recv.at[0])
     total = lax.fori_loop(0, 16, unpack_half(h), jnp.zeros((8, 1024), F32))
-    lax.fori_loop(1, 8, ring_wait, 2)
+    take(pg.at[pl.ds(0, 14)], ring_recv.at[1])
     total = lax.fori_loop(0, 16, unpack_half(1 - h), total)
     pfac[...] = jnp.broadcast_to(
         lax.rsqrt(jnp.sum(total, axis=0, keepdims=True) + EPSILON), (8, 1024)
@@ -238,20 +213,17 @@
     ring_order = (4, 5, 3, 6, 2, 7, 1)
     cx_order = (4, 5, 2, 3, 6, 7, 1)
 
-    def tile_copy(buf, send, recv, device, d):
-        return pltpu.make_async_remote_copy(
-            buf.at[0], buf.at[d], send.at[d], recv, device_id=device, device_id_type=MESH
-        )
-
-    def tile_send(buf, send, recv, group):
+    def tile_send(buf, it, m, send, recv, group):
         devices, order = group
         for d in order:
-            tile_copy(buf, send, recv, devices[d], d).start()
-        drain(1, 8, lambda d: tile_copy(buf, send, recv, core_dev, d))
-
-    def tile_recv(buf, recv):
-        pltpu.make_async_copy(buf.at[pl.ds(1, 7)], buf.at[pl.ds(1, 7)], recv).wait()
-        return jnp.sum(buf[...], axis=0)
+            pltpu.make_async_remote_copy(
+                buf.at[0, it, m], buf.at[d, it, m], send, recv.at[it, m],
+                device_id=devices[d], device_id_type=MESH,
+            ).start()
+
+    def tile_recv(buf, it, m, recv):
+        take(buf.at[pl.ds(1, 7), it, m], recv.at[it, m])
+        return jnp.sum(buf[:, it, m], axis=0)
 
     z_group = ([z_dev(d) for d in range(8)], ring_order)
     y_group = ([y_dev(d) for d in range(8)], ring_order)
@@ -261,7 +233,7 @@
         width = sums.shape[1] // 128
         for part in range(width):
             row = tile * width + part
-            colbuf[it, m, 0, row : row + 1, :] = sums[:, part * 128 : part * 128 + 128]
+            colbuf[0, it, m, row : row + 1, :] = sums[:, part * 128 : part * 128 + 128]
 
     def lane_sums(block):
         return jnp.sum(block.T, axis=0, keepdims=True)
@@ -270,7 +242,7 @@
         return jnp.broadcast_to(row, (128, 128)).T
 
     def col_send_start(it, m):
-        tile_send(colbuf.at[it, m], col_send.at[it, m], col_recv.at[it, m], z_group)
+        tile_send(colbuf, it, m, col_send, col_recv, z_group)
 
     for m in range(2):
         for tile in range(4):
@@ -280,16 +252,6 @@
             kmat[m, :, at] = values
             col_store(0, m, tile, jnp.sum(values, axis=0, keepdims=True))
         col_send_start(0, m)
-
-    for copy in quad_copies:
-        copy.wait_send()
-
-    def ring_sent(d, carry):
-        for j in range(4):
-            ring_copy(j, d).wait_send()
-        return carry
-
-    lax.fori_loop(1, 8, ring_sent, 0)
 
     rows_arrive(sx, sx_send, sx_recv)
     for m in range(2):
@@ -314,25 +276,21 @@
             half = values[:, :128] + values[:, 128:]
             acc = half if acc is None else acc + half
         for part in range(4):
-            rowbuf1[0, m, 0, 4 + part : 5 + part, :] = lane_sums(acc[part * 128 : part * 128 + 128, :])
-
-    load_scale.wait()
-    loss_factor = scale_ref[0] * (1.0 / (2 * 4096 * 0.1))
+            rowbuf1[0, 0, m, 4 + part : 5 + part, :] = lane_sums(acc[part * 128 : part * 128 + 128, :])
 
     for it in range(ITERS):
         for m in range(2):
-            total = tile_recv(colbuf.at[it, m], col_recv.at[it, m])
+            total = tile_recv(colbuf, it, m, col_recv)
             csc[m] = 1.0 / total
             for part in range(4):
                 at = slice(part * 128, part * 128 + 128)
                 acc = jnp.zeros((128, 128), F32)
                 for tile in range(8):
                     acc = acc + kmat[m, at, tile * 128 : tile * 128 + 128] * csc[m, tile : tile + 1, :]
-                rowbuf1[it, m, 0, part : part + 1, :] = lane_sums(acc)
+                rowbuf1[0, it, m, part : part + 1, :] = lane_sums(acc)
             if it > 0:
-                rowbuf1[it, m, 0, 4:8, :] = jnp.zeros((4, 128), F32)
-            tile_send(rowbuf1.at[it, m], row1_send.at[it, m], row1_recv.at[it, m], cx_group)
-        flush()
+                rowbuf1[0, it, m, 4:8, :] = jnp.zeros((4, 128), F32)
+            tile_send(rowbuf1, it, m, row1_send, row1_recv, cx_group)
         if it == 1:
             for m in range(2):
                 for tile in range(8):
@@ -344,18 +302,16 @@
                     at = slice(tile * 128, tile * 128 + 128)
                     kmat[m, :, at] = kmat[m, :, at] * csc[m, tile : tile + 1, :]
         for m in range(2):
-            total = tile_recv(rowbuf1.at[it, m], row1_recv.at[it, m])
-            rowbuf2[it, m, 0] = total
-            tile_send(rowbuf2.at[it, m], row2_send.at[it, m], row2_recv.at[it, m], y_group)
+            total = tile_recv(rowbuf1, it, m, row1_recv)
+            rowbuf2[0, it, m] = total
+            tile_send(rowbuf2, it, m, row2_send, row2_recv, y_group)
         for m in range(2):
-            total = tile_recv(rowbuf2.at[it, m], row2_recv.at[it, m])
+            total = tile_recv(rowbuf2, it, m, row2_recv)
             inverse = 1.0 / total[0:4, :]
-            if it == ITERS - 1:
-                inverse = inverse * loss_factor
             for part in range(4):
                 rb[m, part * 128 : part * 128 + 128, :] = spread(inverse[part : part + 1, :])
             if it == 0:
-                denominator = loss_factor / total[4:8, :]
+                denominator = 1.0 / total[4:8, :]
                 for part in range(4):
                     tb[m, part * 128 : part * 128 + 128, :] = spread(denominator[part : part + 1, :])
             if it < ITERS - 1:
@@ -397,7 +353,7 @@
 
     def rr_copy(i):
         return pltpu.make_async_remote_copy(
-            send_r.at[i], rr.at[me], rr_send.at[i], rr_recv.at[i],
+            send_r.at[i], rr.at[me], rr_send, rr_recv,
             device_id=(back_to(i), mp), device_id_type=MESH,
         )
 
@@ -409,7 +365,6 @@
         return carry
 
     lax.fori_loop(0, 31, send_back, 0)
-    drain(0, 31, rr_copy)
     own = pterm[pl.ds(pl.multiple_of(me * 8, 8), 8), :]
     rr[pl.ds(me, 1)] = jnp.concatenate([own[:, :512], own[:, 512:]], axis=0).astype(BF16)[None]
 
@@ -428,7 +383,7 @@
     def fs_copy(i):
         slot = lax.rem(x + i // 2, 4) * 2 + lax.rem(c + lax.rem(i, 2), 2)
         return pltpu.make_async_remote_copy(
-            fs.at[slot], fr.at[i], fr_send.at[i], fr_recv.at[i],
+            fs.at[slot], fr.at[i], fr_send, fr_recv,
             device_id=cx_dev(i), device_id_type=MESH,
         )
 
@@ -436,14 +391,9 @@
         fs_copy(i).start()
         return carry
 
-    def fs_wait(i, carry):
-        fs_copy(i).wait_recv()
-        return carry
-
     lax.fori_loop(1, 8, fs_start, 0)
-    drain(1, 8, fs_copy)
     fr[pl.ds(0, 1)] = fs[pl.ds(x * 2 + c, 1)]
-    lax.fori_loop(1, 8, fs_wait, 0)
+    take(fr.at[pl.ds(1, 7)], fr_recv)
 
     def fs_sum(l_to, carry):
         at = pl.ds(pl.multiple_of(l_to * 16, 16), 16)
@@ -459,7 +409,7 @@
 
     def gr_copy(d):
         return pltpu.make_async_remote_copy(
-            gsend.at[lax.rem(y + d, 8)], grecv.at[d], gr_send.at[d], gr_recv.at[d],
+            gsend.at[lax.rem(y + d, 8)], grecv.at[d], gr_send, gr_recv,
             device_id=y_dev(d), device_id_type=MESH,
         )
 
@@ -467,34 +417,31 @@
         gr_copy(d).start()
         return carry
 
-    def gr_wait(d, carry):
-        gr_copy(d).wait_recv()
-        return carry
-
     lax.fori_loop(1, 8, gr_start, 0)
-    drain(1, 8, gr_copy)
     grecv[pl.ds(0, 1)] = gsend[pl.ds(y, 1)]
-    lax.fori_loop(1, 8, gr_wait, 0)
+    take(grecv.at[pl.ds(1, 7)], gr_recv)
     total = jnp.sum(grecv[...].astype(F32), axis=0)
     for m in range(2):
         gs_ref[m] = (
             total[:, m * 128 : m * 128 + 128] * sfac[m, pl.ds(q, 1)][0, 0:1, :]
         )
 
-    def rr_wait(d, carry):
-        rr_copy(d).wait_recv()
-        return carry
-
-    flush()
-    lax.fori_loop(0, 31, rr_wait, 0)
+    take(pg.at[pl.ds(0, 31)], pg_send)
+    take(tx.at[:, pl.ds(0, 3)], tx_send)
+    take(sx.at[:, pl.ds(0, 3)], sx_send)
+    take(colbuf.at[pl.ds(1, 7)], col_send)
+    take(rowbuf1.at[pl.ds(1, 7)], row1_send)
+    take(rowbuf2.at[pl.ds(1, 7)], row2_send)
+    take(fr.at[pl.ds(1, 7)], fr_send)
+    take(grecv.at[pl.ds(1, 7)], gr_send)
+    take(rr.at[pl.ds(0, 31)], rr_send)
+    take(rr.at[pl.ds(0, 31)], rr_recv)
     for part in range(4):
         total = rr[part].astype(F32)
         for zz in range(1, 8):
             total = total + rr[zz * 4 + part].astype(F32)
         gp_ref[:, part * 1024 : part * 1024 + 512] = total[0:8, :]
         gp_ref[:, part * 1024 + 512 : part * 1024 + 1024] = total[8:16, :]
-
-    flush()
 
 
 def local(student_patches, teacher_patches, positions, prototypes, loss_scale):
@@ -507,14 +454,13 @@
             pltpu.VMEM((2, 16, 128), F32),
             pltpu.VMEM((8, 4096), F32),
         ),
-        in_specs=[hbm] * 5,
+        in_specs=[hbm] * 4,
         out_specs=(vmem, vmem),
         scratch_shapes=[
             pltpu.VMEM((2, 2, 256, 256), BF16),
             pltpu.VMEM((2, 2, 256, 256), BF16),
             pltpu.VMEM((2, 2, 64), jnp.int32),
             pltpu.VMEM((8, 4096), BF16),
-            pltpu.SMEM((1,), F32),
             pltpu.VMEM((4, 16, 512), BF16),
             pltpu.VMEM((32, 16, 512), BF16),
             pltpu.VMEM((256, 1024), F32),
@@ -530,9 +476,9 @@
             pltpu.VMEM((2, 512, 1024), F32),
             pltpu.VMEM((2, 512, 1024), F32),
             pltpu.VMEM((2, 512, 1024), BF16),
-            pltpu.VMEM((ITERS, 2, 8, 8, 128), F32),
-            pltpu.VMEM((ITERS, 2, 8, 8, 128), F32),
-            pltpu.VMEM((ITERS, 2, 8, 8, 128), F32),
+            pltpu.VMEM((8, ITERS, 2, 8, 128), F32),
+            pltpu.VMEM((8, ITERS, 2, 8, 128), F32),
+            pltpu.VMEM((8, ITERS, 2, 8, 128), F32),
             pltpu.VMEM((2, 8, 128), F32),
             pltpu.VMEM((2, 512, 128), F32),
             pltpu.VMEM((2, 512, 128), F32),
@@ -543,25 +489,26 @@
             pltpu.VMEM((8, 64, 512), BF16),
             pltpu.VMEM((8, 16, 256), BF16),
             pltpu.VMEM((8, 16, 256), BF16),
-            dma((5,)),
-            dma((32,)),
-            dma((32,)),
-            dma((9,)),
-            dma((9,)),
-            dma((9,)),
-            dma((9,)),
-            dma((ITERS, 2, 8)),
+            dma((4,)),
+            dma(()),
+            dma((4,)),
+            dma((2,)),
+            dma(()),
+            dma((3,)),
+            dma(()),
+            dma((3,)),
+            dma(()),
             dma((ITERS, 2)),
-            dma((ITERS, 2, 8)),
+            dma(()),
             dma((ITERS, 2)),
-            dma((ITERS, 2, 8)),
+            dma(()),
             dma((ITERS, 2)),
-            dma((32,)),
-            dma((32,)),
-            dma((8,)),
-            dma((8,)),
-            dma((8,)),
-            dma((8,)),
+            dma(()),
+            dma(()),
+            dma(()),
+            dma(()),
+            dma(()),
+            dma(()),
         ],
         compiler_params=pltpu.CompilerParams(
             collective_id=0, has_side_effects=True, vmem_limit_bytes=60 * 2**20
@@ -570,8 +517,9 @@
             flops=2_200_000_000, bytes_accessed=2_000_000, transcendentals=2_000_000
         ),
         name="ibot_head",
-    )(student_patches, teacher_patches, positions, prototypes, loss_scale)
-    return jnp.transpose(grad_t, (0, 2, 1)), grad_protos
+    )(student_patches, teacher_patches, positions, prototypes)
+    factor = loss_scale[0] * (1.0 / (2 * 4096 * 0.1))
+    return jnp.transpose(grad_t, (0, 2, 1)) * factor, grad_protos * factor
 
 
 def solution(mesh):

time: 92.2 us -> 89.3 us (0.969)
  Pallas kernels: 89.5 us -> 86.6 us
  other arithmetic: 0 us -> 1.28 us
  local copies, waits for them, and re-layouts: 1.26 us -> 0 us
    pallas_call x1, Pallas kernels: 89.5 us -> 86.6 us  [local(): pl.pallas_call(kernel, out_shape=(pltpu.VMEM((2, 16, 128), F32), pltpu.VM...]
    mul x0 -> x2, other arithmetic: none -> 1.28 us  [local(): return (jnp.transpose(grad_t, (0, 2, 1)) * factor, grad_protos * factor)]
    unnamed x2 -> x0, local copies, waits for them, and re-layouts: 1.26 us -> none
where the time goes in v4:
time: 89.3 us; the launch traced here: 89.1 us
  Pallas kernels  86.6 us (97%)
  between operations  1.29 us (1%)
  other arithmetic  1.28 us (1%)
    pallas_call x1, Pallas kernels, local(): pl.pallas_call(kernel, out_shape=(pltpu.VMEM((2, 16, 128), F32), pltpu.VM...  86.6 us

profile of v4, /device:TPU:1, one launch (start us, length us, event | category | flops | bytes accessed | tf_op | source)
XLA Modules:
  0.0 89.1 jit_solution(12652378984446465370)
XLA Ops:
  1.3 86.6 %ibot_head.1 = (f32[2,16,128]{2,1,0:T(8,128)S(1)}, f32[8,4096]{1,0:T(8,128)S(1)}) custom-call(bf16[2,2,256,256]{3,2,1,0:T(8,128)(2,1)} %sp_hbm.1, bf16[2,2,256,256]{3,2,1,0:T(8,128)(2,1)} %tp_hbm.1, s32[2,2,64]{2,1,0:T(2,128)} %pos_hbm.1, bf16[8,4096]{1,0:T(8,128)(2,1)} %pr_hbm.1), custom_call_target="tpu_custom_call" | custom-call | flops 2200000000 | bytes 2000000 | tf_op jit(solution)/shard_map/ibot_head/pallas_call | solution.py:451
  87.9 0.6 multiply_bitcast_fusion
  88.5 0.7 broadcast_multiply_fusion

commit v5 on v4

--- a/solution.py
+++ b/solution.py
@@ -113,6 +113,8 @@
     for copy in quad_copies:
         copy.start()
     ring_start(0)
+    quad_copies[2].wait_recv()
+    ring_start(1)
 
     def pick(patches, m):
         parts = []
@@ -149,8 +151,6 @@
         tx[m, pl.ds(q, 1)] = pick(tp, m)[None]
     y4_copy(tx, tx_send, tx_recv).start()
     core_copy(tx, tx_send, tx_recv).start()
-    quad_copies[2].wait_recv()
-    ring_start(1)
     load_s.wait()
     for m in range(2):
         sx[m, pl.ds(q, 1)] = pick(sp, m)[None]
@@ -321,14 +321,15 @@
                     col_store(it + 1, m, tile, sums)
                 col_send_start(it + 1, m)
 
-    for m in range(2):
-        for tile in range(8):
-            at = slice(tile * 128, tile * 128 + 128)
-            slopes[m, :, at] = (emat[m, :, at] - kmat[m, :, at] * rb[m]).astype(BF16)
-
     for tile in range(4):
         at = slice(tile * 256, tile * 256 + 256)
-        proto_sum = dot(sht[0], slopes[0, :, at], 1, 0) + dot(sht[1], slopes[1, :, at], 1, 0)
+        proto_sum = None
+        for m in range(2):
+            scale = jnp.concatenate([rb[m]] * 2, axis=1)
+            values = (emat[m, :, at] - kmat[m, :, at] * scale).astype(BF16)
+            slopes[m, :, at] = values
+            term = dot(sht[m], values, 1, 0)
+            proto_sum = term if proto_sum is None else proto_sum + term
         unit = pu[:, at]
         column_dot = jnp.sum(unit * proto_sum, axis=0, keepdims=True)
         pterm[:, at] = (proto_sum - unit * column_dot) * pfac[0:1, at]

time: 89.3 us -> 89.3 us (level)
  no operation moved by 1% of the time
where the time goes in v5:
time: 89.3 us; the launch traced here: 89.2 us
  Pallas kernels  86.6 us (97%)
  between operations  1.29 us (1%)
  other arithmetic  1.28 us (1%)
    pallas_call x1, Pallas kernels, local(): pl.pallas_call(kernel, out_shape=(pltpu.VMEM((2, 16, 128), F32), pltpu.VM...  86.6 us

profile of v5, /device:TPU:1, one launch (start us, length us, event | category | flops | bytes accessed | tf_op | source)
XLA Modules:
  0.0 89.2 jit_solution(5374245786933183657)
XLA Ops:
  1.3 86.6 %ibot_head.1 = (f32[2,16,128]{2,1,0:T(8,128)S(1)}, f32[8,4096]{1,0:T(8,128)S(1)}) custom-call(bf16[2,2,256,256]{3,2,1,0:T(8,128)(2,1)} %sp_hbm.1, bf16[2,2,256,256]{3,2,1,0:T(8,128)(2,1)} %tp_hbm.1, s32[2,2,64]{2,1,0:T(2,128)} %pos_hbm.1, bf16[8,4096]{1,0:T(8,128)(2,1)} %pr_hbm.1), custom_call_target="tpu_custom_call" | custom-call | flops 2200000000 | bytes 2000000 | tf_op jit(solution)/shard_map/ibot_head/pallas_call | solution.py:452
  87.9 0.6 multiply_bitcast_fusion
  88.5 0.7 broadcast_multiply_fusion
